TPU v7x, 512 devices: a whole 4x8x8 slice. The times are simulated.
512 devices in a mesh: stream: 16 (over x_lo, z), cross: 32 (over y, x_hi, core).
Axes of the slice: x: 4 (x_hi: 2, x_lo: 2; x = x_hi * 2 + x_lo), y: 8, z: 8, core: 2. Of those that a mesh axis runs over, the one named last changes fastest.
Arguments:
- state_field: float32 [5, 64, 256, 512], P(None, 'stream', 'cross'), may hold values from -0.6 to 4, as said below
- diag_inverse: float32 [25, 64, 256, 512], P(None, 'stream', 'cross'), may hold values from -0.08 to 1.3, as said below
- boundary_low: int32 [64, 512], P('stream'), may hold values from 0 to 2
- boundary_high: int32 [64, 512], P('stream'), may hold values from 0 to 2
Outputs:
- residual: float32 [5, 64, 256, 512], P(None, 'stream', 'cross')
- update: float32 [5, 64, 256, 512], P(None, 'stream', 'cross')
Inputs may be any that keep to these rules, and one draw needn't show every extreme that they name: `boundary_low`: entries of 0 mean slip walls, 1 extrapolation, 2 free stream. `boundary_high`: entries of 0 mean slip walls, 1 extrapolation, 2 free stream. `state_field`: density lies between 0.7 and 1.4, streamwise velocity between -0.05 and 0.05, the other velocities between -0.4 and 0.4, pressure between 0.6 and 1.4. `diag_inverse`: entries on each block's diagonal are positive.
All inputs are finite; a program needn't handle non-finite values.
Results may differ from a plain program's by a relative error of at most 0.0003.
Values sent between devices are 32-bit elements; how exact they have to be, the bound alone decides.
A program may use at most 64 MiB of HBM per device.

v0:
```python
import functools

import jax
import jax.numpy as jnp
from jax import lax
from jax.experimental import pallas as pl
from jax.experimental.pallas import tpu as pltpu
from jax.sharding import PartitionSpec as P

MESH = pl.DeviceIdType.MESH
free_values = (1.0, 0.0, 0.0, 0.0, 2.5)
CHUNK = 128
RHO, U1, U2, U3, PRES, ENTH, ROOT = range(7)


def primitive(q):
    inv_root = lax.rsqrt(q[0])
    inv = inv_root * inv_root
    u = [q[1] * inv, q[2] * inv, q[3] * inv]
    pressure = 0.4 * (q[4] - 0.5 * (q[1] * u[0] + q[2] * u[1] + q[3] * u[2]))
    return [q[0], *u, pressure, (q[4] + pressure) * inv, q[0] * inv_root]


def roe_twice(left, right, d):
    share = right[ROOT] / (left[ROOT] + right[ROOT])
    jump = [right[1 + k] - left[1 + k] for k in range(3)]
    avg = [left[1 + k] + share * jump[k] for k in range(3)]
    enth = left[ENTH] + share * (right[ENTH] - left[ENTH])
    kinetic = 0.5 * (avg[0] * avg[0] + avg[1] * avg[1] + avg[2] * avg[2])
    sound_sq = 0.4 * (enth - kinetic)
    inv_sound = lax.rsqrt(sound_sq)
    sound = sound_sq * inv_sound
    inv_sq = inv_sound * inv_sound
    dens = left[ROOT] * right[ROOT]
    normal = avg[d]
    scaled_pres = (right[PRES] - left[PRES]) * inv_sq
    scaled_jump = dens * inv_sound * jump[d]
    slow = jnp.abs(normal - sound) * (0.5 * (scaled_pres - scaled_jump))
    fast = jnp.abs(normal + sound) * (0.5 * (scaled_pres + scaled_jump))
    speed = jnp.abs(normal)
    entropy = speed * (right[RHO] - left[RHO] - scaled_pres)
    shear = speed * dens
    acoustic = slow + fast
    total = acoustic + entropy
    spread = (fast - slow) * sound
    mass_left = left[RHO] * left[1 + d]
    mass_right = right[RHO] * right[1 + d]
    pieces = [mass_left + mass_right - total]
    along = 0.0
    for k in range(3):
        central = mass_left * left[1 + k] + mass_right * right[1 + k]
        if k == d:
            pieces.append(central + (left[PRES] + right[PRES]) - (total * avg[k] + spread))
        else:
            pieces.append(central - (total * avg[k] + shear * jump[k]))
            along = along + avg[k] * jump[k]
    pieces.append(
        mass_left * left[ENTH]
        + mass_right * right[ENTH]
        - (acoustic * enth + spread * normal + entropy * kinetic + shear * along)
    )
    return pieces


def half_jacobian(w):
    u, v, s = 0.5 * w[U1], 0.5 * w[U2], 0.5 * w[U3]
    phi = 0.1 * (w[U1] * w[U1] + w[U2] * w[U2] + w[U3] * w[U3])
    inv_root = w[ROOT] / w[RHO]
    pos = 1.4 * w[PRES]
    lam = jnp.abs(u) + 0.5 * (pos * lax.rsqrt(pos) * inv_root)
    return u, v, s, phi, 0.5 * w[ENTH], lam, w[U1], w[U2], w[U3]


def row_times(row, jac, sign):
    u, v, s, phi, enth, lam, u1, _, _ = jac
    pres = row[1] + u1 * row[4]
    move = u * row[1] + v * row[2] + s * row[3] + enth * row[4]
    own = u + sign * lam
    return [
        phi * pres - u1 * move + (sign * lam) * row[0],
        0.5 * row[0] + own * row[1] + move - 0.4 * (u * pres),
        own * row[2] - 0.4 * (v * pres),
        own * row[3] - 0.4 * (s * pres),
        own * row[4] + 0.2 * pres,
    ]


def mat_vec(load, vec):
    out = []
    for r in range(5):
        total = load(5 * r) * vec[0]
        for k in range(1, 5):
            total = total + load(5 * r + k) * vec[k]
        out.append(total)
    return out


def kernel(
    streams, crosses,
    state, diag_hbm, kinds_low, kinds_high, res_hbm, upd_hbm,
    diag, prim, edge, halo_cross, halo_stream, low_prim, top_flux,
    flux_stream, res, drive, mats_f, mats_b, prod_f, prod_b, base, upd,
    f_in, f_out, b_in, b_out,
    diag_sem, out_sem, halo_send, halo_recv, f_send, f_recv, b_send, b_recv,
):
    me = lax.axis_index("stream")
    mine = lax.axis_index("cross")
    planes, rows, lanes = state.shape[1:]
    chunks = lanes // CHUNK
    up = {"stream": lax.rem(me + 1, streams)}
    down = {"stream": lax.rem(me + streams - 1, streams)}
    high = {"cross": lax.rem(mine + 1, crosses)}
    low = {"cross": lax.rem(mine + crosses - 1, crosses)}

    load_diag = pltpu.make_async_copy(diag_hbm, diag, diag_sem)
    load_diag.start()
    barrier = pltpu.get_barrier_semaphore()
    for to in (up, down, high, low):
        pl.semaphore_signal(barrier, inc=1, device_id=to, device_id_type=MESH)

    for p in range(planes):
        for k in range(5):
            edge[0, k, pl.ds(p, 1), :] = state[k, p, pl.ds(0, 1), :]
            edge[1, k, pl.ds(p, 1), :] = state[k, p, pl.ds(rows - 1, 1), :]
    pl.semaphore_wait(barrier, 4)

    def remote(src, dst, send, recv, to):
        return pltpu.make_async_remote_copy(
            src_ref=src, dst_ref=dst, send_sem=send, recv_sem=recv,
            device_id=to, device_id_type=MESH,
        )

    halos = [
        remote(edge.at[1], halo_cross.at[0], halo_send.at[0], halo_recv.at[0], high),
        remote(edge.at[0], halo_cross.at[1], halo_send.at[1], halo_recv.at[1], low),
        remote(state.at[:, planes - 1], halo_stream.at[0], halo_send.at[2], halo_recv.at[2], up),
        remote(state.at[:, 0], halo_stream.at[1], halo_send.at[3], halo_recv.at[3], down),
    ]
    for copy in halos:
        copy.start()

    def get(ref, index, count):
        return [ref[(k, *index)] for k in range(count)]

    def put(ref, index, values):
        for k, value in enumerate(values):
            ref[(k, *index)] = value

    def own_plane(p, carry):
        cell = primitive(get(state, (p,), 5))
        put(prim, (p + 1,), cell)
        ahead = [pltpu.roll(field, lanes - 1, 1) for field in cell]
        face = roe_twice(cell, ahead, 2)
        put(res, (p,), [f - pltpu.roll(f, 1, 1) for f in face])
        return carry

    lax.fori_loop(0, planes, own_plane, 0)

    def inner_face(f, carry):
        put(flux_stream, (f,), roe_twice(get(prim, (f,), 7), get(prim, (f + 1,), 7), 0))
        return carry

    lax.fori_loop(1, planes, inner_face, 0)

    for copy in halos:
        copy.wait()

    below = [
        jnp.where(me == 0, free_values[k], halo_stream[0, k]) for k in range(5)
    ]
    put(prim, (0,), primitive(below))
    above = [
        jnp.where(me == streams - 1, state[k, planes - 1], halo_stream[1, k]) for k in range(5)
    ]
    put(prim, (planes + 1,), primitive(above))
    lax.fori_loop(0, 2, lambda i, c: inner_face(i * planes, c), 0)

    def ghost(cell, kinds):
        out = []
        for k in range(5):
            mirror = -cell[k] if k == 2 else cell[k]
            out.append(
                jnp.where(kinds == 0, mirror, jnp.where(kinds == 1, cell[k], free_values[k]))
            )
        return out

    first = [edge[0, k] for k in range(5)]
    last = [edge[1, k] for k in range(5)]
    ghost_low = ghost(first, kinds_low[...])
    ghost_high = ghost(last, kinds_high[...])
    side_low = [jnp.where(mine == 0, ghost_low[k], halo_cross[0, k]) for k in range(5)]
    side_high = [
        jnp.where(mine == crosses - 1, ghost_high[k], halo_cross[1, k]) for k in range(5)
    ]
    put(low_prim, (), primitive(side_low))
    put(top_flux, (), roe_twice(primitive(last), primitive(side_high), 1))

    load_diag.wait()
    row_no = lax.broadcasted_iota(jnp.int32, (rows, lanes), 0)

    def plane_residual(p, previous):
        cell = get(prim, (p + 1,), 7)
        under = [
            jnp.where(row_no == 0, low_prim[k, pl.ds(p, 1), :], pltpu.roll(cell[k], 1, 0))
            for k in range(7)
        ]
        face = roe_twice(under, cell, 1)
        total = []
        for k in range(5):
            over = jnp.where(
                row_no == rows - 1,
                top_flux[k, pl.ds(p, 1), :],
                pltpu.roll(face[k], rows - 1, 0),
            )
            total.append(
                0.5
                * (
                    (flux_stream[k, p + 1] - flux_stream[k, p])
                    + (over - face[k])
                    + res[k, p]
                )
            )
        put(res, (p,), total)
        return previous

    lax.fori_loop(0, planes, plane_residual, 0)
    save_res = pltpu.make_async_copy(res, res_hbm, out_sem.at[0])
    save_res.start()

    def plane_drive(p, previous):
        jac = half_jacobian(get(prim, (p,), 7))
        u, v, s, phi, enth, lam, u1, _, _ = jac
        own = u + lam
        q = previous[1] - u1 * previous[0]
        pres = (
            phi * previous[0]
            - 0.4 * (u * previous[1] + v * previous[2] + s * previous[3])
            + 0.2 * previous[4]
        )
        term = [
            0.5 * previous[1] + lam * previous[0],
            own * previous[1] + u * q + pres,
            own * previous[2] + v * q,
            own * previous[3] + s * q,
            own * previous[4] + u1 * pres + enth * q,
        ]
        vec = [term[k] - res[k, p] for k in range(5)]
        out = mat_vec(lambda e: diag[e, p], vec)
        put(drive, (p,), out)
        return tuple(out)

    zero = jnp.zeros((rows, lanes), jnp.float32)
    lax.fori_loop(0, planes, plane_drive, (zero,) * 5)

    def spot(c):
        return pl.ds(pl.multiple_of(c * CHUNK, CHUNK), CHUNK)

    def f_copy(c):
        return remote(f_out.at[c], f_in.at[c], f_send.at[c], f_recv.at[c], up)

    def b_copy(c):
        return remote(b_out.at[c], b_in.at[c], b_send.at[c], b_recv.at[c], down)

    @pl.when(me == 0)
    def _():
        def start(c, carry):
            for k in range(5):
                f_out[c, k] = drive[k, planes - 1, :, spot(c)]
            f_copy(c).start()
            return carry

        lax.fori_loop(0, chunks, start, 0)

    def matrices(p, carry):
        jac_low = half_jacobian(get(prim, (p,), 7))
        jac_high = half_jacobian(get(prim, (p + 2,), 7))
        for r in range(5):
            row = [diag[5 * r + k, p] for k in range(5)]
            for k, value in enumerate(row_times(row, jac_low, 1.0)):
                mats_f[5 * r + k, p] = value
            minus = [-value for value in row]
            for k, value in enumerate(row_times(minus, jac_high, -1.0)):
                mats_b[5 * r + k, p] = value
        return carry

    lax.fori_loop(0, planes, matrices, 0)

    def multiply(mats, prod, p):
        def column(j, carry):
            vec = [prod[5 * k + j] for k in range(5)]
            for r, value in enumerate(mat_vec(lambda e: mats[e, p], vec)):
                prod[5 * r + j] = value
            return carry

        lax.fori_loop(0, 5, column, 0)

    def start_product(mats, prod, p):
        def entry(e, carry):
            prod[e] = mats[e, p]
            return carry

        lax.fori_loop(0, 25, entry, 0)

    start_product(mats_f, prod_f, 0)
    lax.fori_loop(1, planes, lambda p, c: (multiply(mats_f, prod_f, p), c)[1], 0)

    def settle(c):
        at = spot(c)
        delta = [jnp.where(me == 0, 0.0, f_in[c, k]) for k in range(5)]
        star = []
        for p in range(planes):
            delta = mat_vec(lambda e: mats_f[e, p, :, at], delta)
            star.append([drive[k, p, :, at] + delta[k] for k in range(5)])
        current = star[planes - 1]
        for p in reversed(range(planes)):
            if p < planes - 1:
                step = mat_vec(lambda e: mats_b[e, p, :, at], current)
                current = [star[p][k] + step[k] for k in range(5)]
            for k in range(5):
                base[k, p, :, at] = current[k]
        return current

    def f_relay(c, carry):
        f_copy(c).wait_recv()
        at = spot(c)
        step = mat_vec(lambda e: prod_f[e, :, at], [f_in[c, k] for k in range(5)])
        for k in range(5):
            f_out[c, k] = drive[k, planes - 1, :, at] + step[k]
        f_copy(c).start()
        return carry

    @pl.when((me > 0) & (me < streams - 1))
    def _():
        lax.fori_loop(0, chunks, f_relay, 0)

    @pl.when(me < streams - 1)
    def _():
        lax.fori_loop(0, chunks, lambda c, carry: (settle(c), carry)[1], 0)
        start_product(mats_b, prod_b, planes - 1)
        lax.fori_loop(
            1, planes, lambda i, carry: (multiply(mats_b, prod_b, planes - 1 - i), carry)[1], 0
        )

    @pl.when(me == streams - 1)
    def _():
        def turn(c, carry):
            f_copy(c).wait_recv()
            current = settle(c)
            for k in range(5):
                b_out[c, k] = current[k]
            b_copy(c).start()
            return carry

        lax.fori_loop(0, chunks, turn, 0)

    def b_relay(c, carry):
        b_copy(c).wait_recv()
        at = spot(c)
        step = mat_vec(lambda e: prod_b[e, :, at], [b_in[c, k] for k in range(5)])
        for k in range(5):
            b_out[c, k] = base[k, 0, :, at] + step[k]
        b_copy(c).start()
        return carry

    @pl.when((me > 0) & (me < streams - 1))
    def _():
        lax.fori_loop(0, chunks, b_relay, 0)

    def finish(c, carry):
        at = spot(c)
        delta = [jnp.where(me == streams - 1, 0.0, b_in[c, k]) for k in range(5)]
        for p in reversed(range(planes)):
            delta = mat_vec(lambda e: mats_b[e, p, :, at], delta)
            for k in range(5):
                upd[k, p, :, at] = base[k, p, :, at] + delta[k]
        return carry

    @pl.when(me > 0)
    def _():
        lax.fori_loop(0, chunks, finish, 0)

    @pl.when(me == 0)
    def _():
        def last_step(c, carry):
            b_copy(c).wait_recv()
            return finish(c, carry)

        lax.fori_loop(0, chunks, last_step, 0)

    save_upd = pltpu.make_async_copy(upd, upd_hbm, out_sem.at[1])
    save_upd.start()

    @pl.when(me < streams - 1)
    def _():
        lax.fori_loop(0, chunks, lambda c, carry: (f_copy(c).wait_send(), carry)[1], 0)

    @pl.when(me > 0)
    def _():
        lax.fori_loop(0, chunks, lambda c, carry: (b_copy(c).wait_send(), carry)[1], 0)

    save_res.wait()
    save_upd.wait()


def local(streams, crosses, state, diag, kinds_low, kinds_high):
    _, planes, rows, lanes = state.shape
    chunks = lanes // CHUNK
    f32 = jnp.float32
    block = (planes, rows, lanes)

    def vmem(*shape):
        return pltpu.VMEM(shape, f32)

    return pl.pallas_call(
        functools.partial(kernel, streams, crosses),
        out_shape=[jax.ShapeDtypeStruct(state.shape, f32)] * 2,
        in_specs=[
            pl.BlockSpec(memory_space=pltpu.VMEM),
            pl.BlockSpec(memory_space=pl.ANY),
            pl.BlockSpec(memory_space=pltpu.VMEM),
            pl.BlockSpec(memory_space=pltpu.VMEM),
        ],
        out_specs=[pl.BlockSpec(memory_space=pl.ANY)] * 2,
        scratch_shapes=[
            vmem(25, *block),
            vmem(7, planes + 2, rows, lanes),
            vmem(2, 5, planes, lanes),
            vmem(2, 5, planes, lanes),
            vmem(2, 5, rows, lanes),
            vmem(7, planes, lanes),
            vmem(5, planes, lanes),
            vmem(5, planes + 1, rows, lanes),
            vmem(5, *block),
            vmem(5, *block),
            vmem(25, *block),
            vmem(25, *block),
            vmem(25, rows, lanes),
            vmem(25, rows, lanes),
            vmem(5, *block),
            vmem(5, *block),
            vmem(chunks, 5, rows, CHUNK),
            vmem(chunks, 5, rows, CHUNK),
            vmem(chunks, 5, rows, CHUNK),
            vmem(chunks, 5, rows, CHUNK),
            pltpu.SemaphoreType.DMA,
            pltpu.SemaphoreType.DMA((2,)),
            pltpu.SemaphoreType.DMA((4,)),
            pltpu.SemaphoreType.DMA((4,)),
            pltpu.SemaphoreType.DMA((chunks,)),
            pltpu.SemaphoreType.DMA((chunks,)),
            pltpu.SemaphoreType.DMA((chunks,)),
            pltpu.SemaphoreType.DMA((chunks,)),
        ],
        compiler_params=pltpu.CompilerParams(
            collective_id=0, has_side_effects=True, vmem_limit_bytes=40 * 2**20
        ),
        cost_estimate=pl.CostEstimate(
            flops=16000000, bytes_accessed=2700000, transcendentals=100000
        ),
    )(state, diag, kinds_low, kinds_high)


def solution(mesh):
    spec = P(None, "stream", "cross", None)
    return jax.shard_map(
        functools.partial(local, mesh.shape["stream"], mesh.shape["cross"]),
        mesh=mesh,
        in_specs=(spec, spec, P("stream", None), P("stream", None)),
        out_specs=(spec, spec),
        check_vma=False,
    )
```

profile of v0, /device:TPU:56, one launch (start us, length us, event | category | flops | bytes accessed | tf_op | source)
XLA Modules:
  0.0 112.6 jit_solution(4192931096735033170)
XLA Ops:
  0.6 0.0 copy-start
  0.6 1.4 %copy-done = f32[25,4,8,512]{3,2,1,0:T(8,128)S(1)} copy-done((f32[25,4,8,512]{3,2,1,0:T(8,128)S(1)}, f32[25,4,8,512]{3,2,1,0:T(8,128)}, u32[]{:S(2)}) %copy-start) | copy-done | bytes 1638424
  2.1 0.0 copy-start.1
  2.1 1.0 copy-done.1
  3.0 0.0 copy-start.2
  3.0 0.7 copy-done.2
  3.7 0.0 copy-start.3
  3.7 0.7 copy-done.3
  4.4 106.7 %shard_map.59 = (f32[5,4,8,512]{3,2,1,0:T(8,128)S(1)}, f32[5,4,8,512]{3,2,1,0:T(8,128)S(1)}) custom-call(f32[5,4,8,512]{3,2,1,0:T(8,128)S(1)} %copy-done.1, f32[25,4,8,512]{3,2,1,0:T(8,128)S(1)} %copy-done, s32[4,512]{1,0:T(4,128)S(1)} %copy-done.2, s32[4,512]{1,0:T(4,128)S(1)} %copy-done.3), custom_call_target="tpu_custom_call" | custom-call | flops 16000000 | bytes 2700000 | tf_op jit(solution)/shard_map/pallas_call | solution.py:414
  111.2 0.7 copy.8
  111.9 0.7 copy.9
Async XLA Ops:
  0.6 1.4 %copy-start = (f32[25,4,8,512]{3,2,1,0:T(8,128)S(1)}, f32[25,4,8,512]{3,2,1,0:T(8,128)}, u32[]{:S(2)}) copy-start(f32[25,4,8,512]{3,2,1,0:T(8,128)} %diag_hbm.1) | copy-start | bytes 4915204
  2.1 1.0 copy-start.1
  3.0 0.7 copy-start.2
  3.7 0.7 copy-start.3
where the time goes:
time: 113 us
  Pallas kernels  107 us (95%)
  local copies, waits for them, and re-layouts  5.24 us (5%)
    pallas_call x1, Pallas kernels, local(): pl.pallas_call(functools.partial(kernel, streams, crosses), out_shape=[ja...  107 us
    unnamed x10, local copies, waits for them, and re-layouts  5.24 us

commit v1 on v0

v1 whole, which is shorter than its diff:
```python
import functools

import jax
import jax.numpy as jnp
from jax import lax
from jax.experimental import pallas as pl
from jax.experimental.pallas import tpu as pltpu
from jax.sharding import PartitionSpec as P

MESH = pl.DeviceIdType.MESH
free_values = (1.0, 0.0, 0.0, 0.0, 2.5)
CHUNK = 128
RHO, U1, U2, U3, PRES, ENTH, ROOT = range(7)


def primitive(q):
    inv_root = lax.rsqrt(q[0])
    inv = inv_root * inv_root
    u = [q[1] * inv, q[2] * inv, q[3] * inv]
    pressure = 0.4 * (q[4] - 0.5 * (q[1] * u[0] + q[2] * u[1] + q[3] * u[2]))
    return [q[0], *u, pressure, (q[4] + pressure) * inv, q[0] * inv_root]


def roe_twice(left, right, d):
    share = right[ROOT] / (left[ROOT] + right[ROOT])
    jump = [right[1 + k] - left[1 + k] for k in range(3)]
    avg = [left[1 + k] + share * jump[k] for k in range(3)]
    enth = left[ENTH] + share * (right[ENTH] - left[ENTH])
    kinetic = 0.5 * (avg[0] * avg[0] + avg[1] * avg[1] + avg[2] * avg[2])
    sound_sq = 0.4 * (enth - kinetic)
    inv_sound = lax.rsqrt(sound_sq)
    sound = sound_sq * inv_sound
    inv_sq = inv_sound * inv_sound
    dens = left[ROOT] * right[ROOT]
    normal = avg[d]
    scaled_pres = (right[PRES] - left[PRES]) * inv_sq
    scaled_jump = dens * inv_sound * jump[d]
    slow = jnp.abs(normal - sound) * (0.5 * (scaled_pres - scaled_jump))
    fast = jnp.abs(normal + sound) * (0.5 * (scaled_pres + scaled_jump))
    speed = jnp.abs(normal)
    entropy = speed * (right[RHO] - left[RHO] - scaled_pres)
    shear = speed * dens
    acoustic = slow + fast
    total = acoustic + entropy
    spread = (fast - slow) * sound
    mass_left = left[RHO] * left[1 + d]
    mass_right = right[RHO] * right[1 + d]
    pieces = [mass_left + mass_right - total]
    along = 0.0
    for k in range(3):
        central = mass_left * left[1 + k] + mass_right * right[1 + k]
        if k == d:
            pieces.append(central + (left[PRES] + right[PRES]) - (total * avg[k] + spread))
        else:
            pieces.append(central - (total * avg[k] + shear * jump[k]))
            along = along + avg[k] * jump[k]
    pieces.append(
        mass_left * left[ENTH]
        + mass_right * right[ENTH]
        - (acoustic * enth + spread * normal + entropy * kinetic + shear * along)
    )
    return pieces


def half_jacobian(w):
    u, v, s = 0.5 * w[U1], 0.5 * w[U2], 0.5 * w[U3]
    phi = 0.1 * (w[U1] * w[U1] + w[U2] * w[U2] + w[U3] * w[U3])
    inv_root = w[ROOT] / w[RHO]
    pos = 1.4 * w[PRES]
    lam = jnp.abs(u) + 0.5 * (pos * lax.rsqrt(pos) * inv_root)
    return u, v, s, phi, 0.5 * w[ENTH], lam, w[U1], w[U2], w[U3]


def row_times(row, jac, sign):
    u, v, s, phi, enth, lam, u1, _, _ = jac
    pres = row[1] + u1 * row[4]
    move = u * row[1] + v * row[2] + s * row[3] + enth * row[4]
    own = u + sign * lam
    return [
        phi * pres - u1 * move + (sign * lam) * row[0],
        0.5 * row[0] + own * row[1] + move - 0.4 * (u * pres),
        own * row[2] - 0.4 * (v * pres),
        own * row[3] - 0.4 * (s * pres),
        own * row[4] + 0.2 * pres,
    ]


def mat_vec(load, vec):
    out = []
    for r in range(5):
        total = load(5 * r) * vec[0]
        for k in range(1, 5):
            total = total + load(5 * r + k) * vec[k]
        out.append(total)
    return out


def kernel(
    streams, crosses,
    state_hbm, diag_hbm, low_hbm, high_hbm, res_hbm, upd_hbm,
    state, diag, kinds_low, kinds_high, prim, edge, halo_cross, halo_stream, low_prim, top_flux,
    flux_stream, res, drive, mats_f, mats_b, prod, base, upd,
    p_out, p_in, q_out, q_in, a_out, a_in, s_out, s_in, b_out, b_in, u_out, u_in,
    load_sem, save_sem, halo_send, halo_recv, sends, recvs,
):
    me = lax.axis_index("stream")
    mine = lax.axis_index("cross")
    planes, rows, lanes = state.shape[1:]
    chunks = lanes // CHUNK
    piece = rows * chunks // streams
    per_chunk = rows // piece
    last = streams - 1
    up = {"stream": lax.rem(me + 1, streams)}
    down = {"stream": lax.rem(me + last, streams)}
    high = {"cross": lax.rem(mine + 1, crosses)}
    low = {"cross": lax.rem(mine + crosses - 1, crosses)}

    loads = [
        pltpu.make_async_copy(src, dst, load_sem.at[i])
        for i, (src, dst) in enumerate(
            [(state_hbm, state), (diag_hbm, diag), (low_hbm, kinds_low), (high_hbm, kinds_high)]
        )
    ]
    for copy in loads:
        copy.start()
    barrier = pltpu.get_barrier_semaphore()

    def greet(o, carry):
        pl.semaphore_signal(
            barrier, inc=1, device_id={"stream": lax.rem(me + o, streams)}, device_id_type=MESH
        )
        return carry

    lax.fori_loop(1, streams, greet, 0)
    for to in (high, low):
        pl.semaphore_signal(barrier, inc=1, device_id=to, device_id_type=MESH)

    loads[0].wait()
    for p in range(planes):
        for k in range(5):
            edge[0, k, pl.ds(p, 1), :] = state[k, p, pl.ds(0, 1), :]
            edge[1, k, pl.ds(p, 1), :] = state[k, p, pl.ds(rows - 1, 1), :]
    pl.semaphore_wait(barrier, streams + 1)

    def remote(src, dst, send, recv, to):
        return pltpu.make_async_remote_copy(
            src_ref=src, dst_ref=dst, send_sem=send, recv_sem=recv,
            device_id=to, device_id_type=MESH,
        )

    halos = [
        remote(state.at[:, planes - 1], halo_stream.at[0], halo_send.at[0], halo_recv.at[0], up),
        remote(state.at[:, 0], halo_stream.at[1], halo_send.at[1], halo_recv.at[1], down),
        remote(edge.at[1], halo_cross.at[0], halo_send.at[2], halo_recv.at[2], high),
        remote(edge.at[0], halo_cross.at[1], halo_send.at[3], halo_recv.at[3], low),
    ]
    for copy in halos:
        copy.start()

    boxes = [
        (p_out, p_in), (a_out, a_in), (s_out, s_in), (q_out, q_in), (b_out, b_in), (u_out, u_in)
    ]
    MAT_F, VEC_F, BACK_F, MAT_B, VEC_B, BACK_B = range(6)

    def outgoing(kind, to):
        out, into = boxes[kind]
        return remote(
            out.at[to], into.at[me], sends.at[kind, to], recvs.at[kind, me], {"stream": to}
        )

    def wait_from(kind, source):
        out, into = boxes[kind]

        @pl.when(source != me)
        def _():
            remote(
                out.at[source], into.at[source], sends.at[kind, source],
                recvs.at[kind, source], {"stream": source},
            ).wait_recv()

    def send_some(kind, first, end):
        def one(o, carry):
            outgoing(kind, lax.rem(me + o, streams)).start()
            return carry

        lax.fori_loop(first, end, one, 0)

    def keep_own(kind, count):
        out, into = boxes[kind]

        def one(e, carry):
            into[me, e] = out[me, e]
            return carry

        lax.fori_loop(0, count, one, 0)

    def pack(out, e, value):
        for c in range(chunks):
            for i in range(per_chunk):
                out[c * per_chunk + i, e] = value[
                    i * piece : (i + 1) * piece, c * CHUNK : (c + 1) * CHUNK
                ]

    def get(ref, index, count):
        return [ref[(k, *index)] for k in range(count)]

    def put(ref, index, values):
        for k, value in enumerate(values):
            ref[(k, *index)] = value

    def own_plane(p, carry):
        put(prim, (p + 1,), primitive(get(state, (p,), 5)))
        return carry

    lax.fori_loop(0, planes, own_plane, 0)
    loads[1].wait()

    def matrices_f(p, carry):
        jac = half_jacobian(get(prim, (p,), 7))
        for r in range(5):
            row = [diag[5 * r + k, p] for k in range(5)]
            for k, value in enumerate(row_times(row, jac, 1.0)):
                mats_f[5 * r + k, p] = value
        return carry

    def matrices_b(p, carry):
        jac = half_jacobian(get(prim, (p + 2,), 7))
        for r in range(5):
            row = [-diag[5 * r + k, p] for k in range(5)]
            for k, value in enumerate(row_times(row, jac, -1.0)):
                mats_b[5 * r + k, p] = value
        return carry

    def multiply(mats, order, out):
        for n, p in enumerate(order[1:]):
            final = n == len(order) - 2

            def column(j, carry):
                if n == 0:
                    vec = [mats[5 * k + j, order[0]] for k in range(5)]
                else:
                    vec = [prod[5 * k + j] for k in range(5)]
                for r, value in enumerate(mat_vec(lambda e: mats[e, p], vec)):
                    if final:
                        pack(out, 5 * r + j, value)
                    else:
                        prod[5 * r + j] = value
                return carry

            lax.fori_loop(0, 5, column, 0)

    lax.fori_loop(1, planes, matrices_f, 0)
    halos[0].wait_recv()
    halos[1].wait_recv()
    below = [jnp.where(me == 0, free_values[k], halo_stream[0, k]) for k in range(5)]
    put(prim, (0,), primitive(below))
    above = [
        jnp.where(me == last, state[k, planes - 1], halo_stream[1, k]) for k in range(5)
    ]
    put(prim, (planes + 1,), primitive(above))
    matrices_f(0, 0)

    @pl.when((me > 0) & (me < last))
    def _():
        multiply(mats_f, list(range(planes)), p_out)
        send_some(MAT_F, 1, streams)
        keep_own(MAT_F, 25)

    def inner_face(f, carry):
        put(flux_stream, (f,), roe_twice(get(prim, (f,), 7), get(prim, (f + 1,), 7), 0))
        return carry

    lax.fori_loop(0, planes + 1, inner_face, 0)

    def span_plane(p, carry):
        cell = get(prim, (p + 1,), 7)
        ahead = [pltpu.roll(field, lanes - 1, 1) for field in cell]
        face = roe_twice(cell, ahead, 2)
        put(res, (p,), [f - pltpu.roll(f, 1, 1) for f in face])
        return carry

    lax.fori_loop(0, planes, span_plane, 0)
    halos[2].wait_recv()
    halos[3].wait_recv()
    loads[2].wait()
    loads[3].wait()

    def ghost(cell, kinds):
        out = []
        for k in range(5):
            mirror = -cell[k] if k == 2 else cell[k]
            out.append(
                jnp.where(kinds == 0, mirror, jnp.where(kinds == 1, cell[k], free_values[k]))
            )
        return out

    row_first = [edge[0, k] for k in range(5)]
    row_last = [edge[1, k] for k in range(5)]
    ghost_low = ghost(row_first, kinds_low[...])
    ghost_high = ghost(row_last, kinds_high[...])
    side_low = [jnp.where(mine == 0, ghost_low[k], halo_cross[0, k]) for k in range(5)]
    side_high = [
        jnp.where(mine == crosses - 1, ghost_high[k], halo_cross[1, k]) for k in range(5)
    ]
    put(low_prim, (), primitive(side_low))
    put(top_flux, (), roe_twice(primitive(row_last), primitive(side_high), 1))

    row_no = lax.broadcasted_iota(jnp.int32, (rows, lanes), 0)

    def plane_residual(p, carry):
        cell = get(prim, (p + 1,), 7)
        under = [
            jnp.where(row_no == 0, low_prim[k, pl.ds(p, 1), :], pltpu.roll(cell[k], 1, 0))
            for k in range(7)
        ]
        face = roe_twice(under, cell, 1)
        for k in range(5):
            over = jnp.where(
                row_no == rows - 1,
                top_flux[k, pl.ds(p, 1), :],
                pltpu.roll(face[k], rows - 1, 0),
            )
            res[k, p] = 0.5 * (
                (flux_stream[k, p + 1] - flux_stream[k, p]) + (over - face[k]) + res[k, p]
            )
        return carry

    lax.fori_loop(0, planes, plane_residual, 0)
    save_res = pltpu.make_async_copy(res, res_hbm, save_sem.at[0])
    save_res.start()

    def plane_drive(p, previous):
        u, v, s, phi, enth, lam, u1, _, _ = half_jacobian(get(prim, (p,), 7))
        own = u + lam
        q = previous[1] - u1 * previous[0]
        pres = (
            phi * previous[0]
            - 0.4 * (u * previous[1] + v * previous[2] + s * previous[3])
            + 0.2 * previous[4]
        )
        term = [
            0.5 * previous[1] + lam * previous[0],
            own * previous[1] + u * q + pres,
            own * previous[2] + v * q,
            own * previous[3] + s * q,
            own * previous[4] + u1 * pres + enth * q,
        ]
        out = mat_vec(lambda e: diag[e, p], [term[k] - res[k, p] for k in range(5)])
        put(drive, (p,), out)
        return tuple(out)

    zero = jnp.zeros((rows, lanes), jnp.float32)
    ahead = lax.fori_loop(0, planes, plane_drive, (zero,) * 5)
    for k in range(5):
        pack(a_out, k, ahead[k])

    @pl.when(me < last)
    def _():
        send_some(VEC_F, 1, streams)
        keep_own(VEC_F, 5)

    lax.fori_loop(0, planes, matrices_b, 0)
    half = streams // 2

    @pl.when((me > 0) & (me < last))
    def _():
        multiply(mats_b, list(reversed(range(planes))), q_out)
        send_some(MAT_B, 1, half)
        keep_own(MAT_B, 25)

    def hand_back(kind, to, values):
        out, into = boxes[kind]
        for k in range(5):
            out[to, k] = values[k]

        @pl.when(to != me)
        def _():
            outgoing(kind, to).start()

        @pl.when(to == me)
        def _():
            for k in range(5):
                into[me, k] = values[k]

    wait_from(VEC_F, 0)
    current = [a_in[0, k] for k in range(5)]
    hand_back(BACK_F, 1, current)

    def scan_f(j, vec):
        wait_from(MAT_F, j)
        wait_from(VEC_F, j)
        step = mat_vec(lambda e: p_in[j, e], vec)
        out = [a_in[j, k] + step[k] for k in range(5)]
        hand_back(BACK_F, j + 1, out)
        return tuple(out)

    lax.fori_loop(1, last, scan_f, tuple(current))

    @pl.when((me > 0) & (me < last))
    def _():
        send_some(MAT_B, half, streams)

    def spot(c):
        return pl.ds(pl.multiple_of(c * CHUNK, CHUNK), CHUNK)

    def gather(kind, c):
        for i in range(per_chunk):
            wait_from(kind, c * per_chunk + i)

    def joined(into, c, k):
        parts = [into[c * per_chunk + i, k] for i in range(per_chunk)]
        return parts[0] if per_chunk == 1 else jnp.concatenate(parts, axis=0)

    def settle(c, carry):
        at = spot(c)

        @pl.when(me > 0)
        def _():
            gather(BACK_F, c)

        delta = [jnp.where(me == 0, 0.0, joined(s_in, c, k)) for k in range(5)]
        star = []
        for p in range(planes):
            delta = mat_vec(lambda e: mats_f[e, p, :, at], delta)
            star.append([drive[k, p, :, at] + delta[k] for k in range(5)])
        current = star[planes - 1]
        for p in reversed(range(planes)):
            if p < planes - 1:
                step = mat_vec(lambda e: mats_b[e, p, :, at], current)
                current = [star[p][k] + step[k] for k in range(5)]
            for k in range(5):
                base[k, p, :, at] = current[k]
        for i in range(per_chunk):
            to = c * per_chunk + i
            for k in range(5):
                b_out[to, k] = current[k][i * piece : (i + 1) * piece]

            @pl.when((me > 0) & (to != me))
            def _():
                outgoing(VEC_B, to).start()

        return carry

    lax.fori_loop(0, chunks, settle, 0)
    keep_own(VEC_B, 5)

    wait_from(VEC_B, last)
    current = [b_in[last, k] for k in range(5)]
    hand_back(BACK_B, last - 1, current)

    def scan_b(n, vec):
        j = last - n
        wait_from(MAT_B, j)
        wait_from(VEC_B, j)
        step = mat_vec(lambda e: q_in[j, e], vec)
        out = [b_in[j, k] + step[k] for k in range(5)]
        hand_back(BACK_B, j - 1, out)
        return tuple(out)

    lax.fori_loop(1, last, scan_b, tuple(current))

    def finish(c, carry):
        at = spot(c)

        @pl.when(me < last)
        def _():
            gather(BACK_B, c)

        delta = [jnp.where(me == last, 0.0, joined(u_in, c, k)) for k in range(5)]
        for p in reversed(range(planes)):
            delta = mat_vec(lambda e: mats_b[e, p, :, at], delta)
            for k in range(5):
                upd[k, p, :, at] = base[k, p, :, at] + delta[k]
        return carry

    lax.fori_loop(0, chunks, finish, 0)
    save_upd = pltpu.make_async_copy(upd, upd_hbm, save_sem.at[1])
    save_upd.start()

    for copy in halos:
        copy.wait_send()

    def sent(kind):
        def one(o, carry):
            outgoing(kind, lax.rem(me + o, streams)).wait_send()
            return carry

        lax.fori_loop(1, streams, one, 0)

    @pl.when((me > 0) & (me < last))
    def _():
        sent(MAT_F)
        sent(MAT_B)

    @pl.when(me < last)
    def _():
        sent(VEC_F)

    @pl.when(me > 0)
    def _():
        sent(VEC_B)

    def sent_back(t, carry):
        @pl.when(t != me)
        def _():
            outgoing(BACK_F, t).wait_send()

        @pl.when(t - 1 != me)
        def _():
            outgoing(BACK_B, t - 1).wait_send()

        return carry

    lax.fori_loop(1, streams, sent_back, 0)
    save_res.wait()
    save_upd.wait()


def local(streams, crosses, state, diag, kinds_low, kinds_high):
    _, planes, rows, lanes = state.shape
    piece = rows * (lanes // CHUNK) // streams
    f32 = jnp.float32
    block = (planes, rows, lanes)

    def vmem(*shape):
        return pltpu.VMEM(shape, f32)

    return pl.pallas_call(
        functools.partial(kernel, streams, crosses),
        out_shape=[jax.ShapeDtypeStruct(state.shape, f32)] * 2,
        in_specs=[pl.BlockSpec(memory_space=pl.ANY)] * 4,
        out_specs=[pl.BlockSpec(memory_space=pl.ANY)] * 2,
        scratch_shapes=[
            vmem(5, *block),
            vmem(25, *block),
            pltpu.VMEM((planes, lanes), jnp.int32),
            pltpu.VMEM((planes, lanes), jnp.int32),
            vmem(7, planes + 2, rows, lanes),
            vmem(2, 5, planes, lanes),
            vmem(2, 5, planes, lanes),
            vmem(2, 5, rows, lanes),
            vmem(7, planes, lanes),
            vmem(5, planes, lanes),
            vmem(5, planes + 1, rows, lanes),
            vmem(5, *block),
            vmem(5, *block),
            vmem(25, *block),
            vmem(25, *block),
            vmem(25, rows, lanes),
            vmem(5, *block),
            vmem(5, *block),
            *[vmem(streams, 25, piece, CHUNK)] * 4,
            *[vmem(streams, 5, piece, CHUNK)] * 8,
            pltpu.SemaphoreType.DMA((4,)),
            pltpu.SemaphoreType.DMA((2,)),
            pltpu.SemaphoreType.DMA((4,)),
            pltpu.SemaphoreType.DMA((4,)),
            pltpu.SemaphoreType.DMA((6, streams)),
            pltpu.SemaphoreType.DMA((6, streams)),
        ],
        compiler_params=pltpu.CompilerParams(
            collective_id=0, has_side_effects=True, vmem_limit_bytes=60 * 2**20
        ),
        cost_estimate=pl.CostEstimate(
            flops=16000000, bytes_accessed=2700000, transcendentals=100000
        ),
    )(state, diag, kinds_low, kinds_high)


def solution(mesh):
    spec = P(None, "stream", "cross", None)
    return jax.shard_map(
        functools.partial(local, mesh.shape["stream"], mesh.shape["cross"]),
        mesh=mesh,
        in_specs=(spec, spec, P("stream", None), P("stream", None)),
        out_specs=(spec, spec),
        check_vma=False,
    )
```

time: 113 us -> 56.9 us (0.50)
  Pallas kernels: 107 us -> 51.7 us
  local copies, waits for them, and re-layouts: 5.24 us -> 3.45 us
    pallas_call x1, Pallas kernels: 107 us -> 51.7 us  [local(): pl.pallas_call(functools.partial(kernel, streams, crosses), out_shape=[ja...]
    unnamed x10 -> x2, local copies, waits for them, and re-layouts: 5.24 us -> 3.45 us
where the time goes in v1:
time: 56.9 us; the launch traced here: 55.8 us
  Pallas kernels  51.7 us (91%)
  local copies, waits for them, and re-layouts  3.45 us (6%)
  between operations  0.64 us (1%)
    pallas_call x1, Pallas kernels, local(): pl.pallas_call(functools.partial(kernel, streams, crosses), out_shape=[ja...  51.7 us
    unnamed x2, local copies, waits for them, and re-layouts  3.45 us

profile of v1, /device:TPU:56, one launch (start us, length us, event | category | flops | bytes accessed | tf_op | source)
XLA Modules:
  0.0 55.8 jit_solution(17181084135244771434)
XLA Ops:
  0.6 51.7 %shard_map.59 = (f32[5,4,8,512]{3,2,1,0:T(8,128)}, f32[5,4,8,512]{3,2,1,0:T(8,128)}) custom-call(f32[5,4,8,512]{3,2,1,0:T(8,128)} %state_hbm.1, f32[25,4,8,512]{3,2,1,0:T(8,128)} %diag_hbm.1, s32[4,512]{1,0:T(4,128)} %low_hbm.1, s32[4,512]{1,0:T(4,128)} %high_hbm.1), custom_call_target="tpu_custom_call" | custom-call | flops 16000000 | bytes 2700000 | tf_op jit(solution)/shard_map/pallas_call | solution.py:528
  52.3 1.7 %copy.8 = f32[5,4,8,512]{3,2,1,0:T(8,128)} copy(f32[5,4,8,512]{3,2,1,0:T(8,128)} %get-tuple-element.4) | data formatting | bytes 655360
  54.1 1.7 %copy.9 = f32[5,4,8,512]{3,2,1,0:T(8,128)} copy(f32[5,4,8,512]{3,2,1,0:T(8,128)} %get-tuple-element.5) | data formatting | bytes 655360

commit v2 on v1

--- a/solution.py
+++ b/solution.py
@@ -85,23 +85,35 @@
     ]
 
 
+def half_apply(jac, vec, sign):
+    u, v, s, phi, enth, lam, u1, _, _ = jac
+    own = u + sign * lam
+    q = vec[1] - u1 * vec[0]
+    pres = phi * vec[0] - 0.4 * (u * vec[1] + v * vec[2] + s * vec[3]) + 0.2 * vec[4]
+    return [
+        0.5 * vec[1] + (sign * lam) * vec[0],
+        own * vec[1] + u * q + pres,
+        own * vec[2] + v * q,
+        own * vec[3] + s * q,
+        own * vec[4] + u1 * pres + enth * q,
+    ]
+
+
 def mat_vec(load, vec):
     out = []
     for r in range(5):
-        total = load(5 * r) * vec[0]
-        for k in range(1, 5):
-            total = total + load(5 * r + k) * vec[k]
-        out.append(total)
+        term = [load(5 * r + k) * vec[k] for k in range(5)]
+        out.append((term[0] + term[1]) + (term[2] + term[3]) + term[4])
     return out
 
 
 def kernel(
     streams, crosses,
-    state_hbm, diag_hbm, low_hbm, high_hbm, res_hbm, upd_hbm,
-    state, diag, kinds_low, kinds_high, prim, edge, halo_cross, halo_stream, low_prim, top_flux,
-    flux_stream, res, drive, mats_f, mats_b, prod, base, upd,
+    state_hbm, diag_hbm, kinds_hbm, res, upd,
+    state, diag, kinds, prim, edge, halo_cross, halo_stream, low_prim, top_flux,
+    flux_stream, drive, mats_f, mats_b, base,
     p_out, p_in, q_out, q_in, a_out, a_in, s_out, s_in, b_out, b_in, u_out, u_in,
-    load_sem, save_sem, halo_send, halo_recv, sends, recvs,
+    load_sem, halo_send, halo_recv, sends, recvs,
 ):
     me = lax.axis_index("stream")
     mine = lax.axis_index("cross")
@@ -118,7 +130,7 @@
     loads = [
         pltpu.make_async_copy(src, dst, load_sem.at[i])
         for i, (src, dst) in enumerate(
-            [(state_hbm, state), (diag_hbm, diag), (low_hbm, kinds_low), (high_hbm, kinds_high)]
+            [(state_hbm, state), (diag_hbm, diag), (kinds_hbm, kinds)]
         )
     ]
     for copy in loads:
@@ -134,12 +146,68 @@
     lax.fori_loop(1, streams, greet, 0)
     for to in (high, low):
         pl.semaphore_signal(barrier, inc=1, device_id=to, device_id_type=MESH)
+
+    def get(ref, index, count):
+        return [ref[(k, *index)] for k in range(count)]
+
+    def put(ref, index, values):
+        for k, value in enumerate(values):
+            ref[(k, *index)] = value
+
+    def pack(out, e, value):
+        for c in range(chunks):
+            for i in range(per_chunk):
+                out[c * per_chunk + i, e] = value[
+                    i * piece : (i + 1) * piece, c * CHUNK : (c + 1) * CHUNK
+                ]
+
+    def matrices_f(p, carry):
+        jac = half_jacobian(get(prim, (p,), 7))
+        for r in range(5):
+            row = [diag[5 * r + k, p] for k in range(5)]
+            for k, value in enumerate(row_times(row, jac, 1.0)):
+                mats_f[5 * r + k, p] = value
+        return carry
+
+    def matrices_b(p, carry):
+        jac = half_jacobian(get(prim, (p + 2,), 7))
+        for r in range(5):
+            row = [-diag[5 * r + k, p] for k in range(5)]
+            for k, value in enumerate(row_times(row, jac, -1.0)):
+                mats_b[5 * r + k, p] = value
+        return carry
+
+    def product_f(j, carry):
+        vec = [diag[5 * k + j, 0] for k in range(5)]
+        for p in range(1, planes):
+            vec = mat_vec(lambda e: mats_f[e, p], vec)
+        vec = half_apply(half_jacobian(get(prim, (planes,), 7)), vec, 1.0)
+        for r in range(5):
+            pack(p_out, 5 * r + j, vec[r])
+        return carry
+
+    def product_b(j, carry):
+        vec = [-diag[5 * k + j, planes - 1] for k in range(5)]
+        for p in reversed(range(planes - 1)):
+            vec = mat_vec(lambda e: mats_b[e, p], vec)
+        vec = half_apply(half_jacobian(get(prim, (1,), 7)), vec, -1.0)
+        for r in range(5):
+            pack(q_out, 5 * r + j, vec[r])
+        return carry
+
+    def own_plane(p, carry):
+        put(prim, (p + 1,), primitive(get(state, (p,), 5)))
+        return carry
 
     loads[0].wait()
     for p in range(planes):
         for k in range(5):
             edge[0, k, pl.ds(p, 1), :] = state[k, p, pl.ds(0, 1), :]
             edge[1, k, pl.ds(p, 1), :] = state[k, p, pl.ds(rows - 1, 1), :]
+    lax.fori_loop(0, planes, own_plane, 0)
+    loads[1].wait()
+    lax.fori_loop(1, planes, matrices_f, 0)
+    lax.fori_loop(0, 5, product_f, 0)
     pl.semaphore_wait(barrier, streams + 1)
 
     def remote(src, dst, send, recv, to):
@@ -185,6 +253,13 @@
 
         lax.fori_loop(first, end, one, 0)
 
+    def sent(kind):
+        def one(o, carry):
+            outgoing(kind, lax.rem(me + o, streams)).wait_send()
+            return carry
+
+        lax.fori_loop(1, streams, one, 0)
+
     def keep_own(kind, count):
         out, into = boxes[kind]
 
@@ -194,62 +269,25 @@
 
         lax.fori_loop(0, count, one, 0)
 
-    def pack(out, e, value):
-        for c in range(chunks):
-            for i in range(per_chunk):
-                out[c * per_chunk + i, e] = value[
-                    i * piece : (i + 1) * piece, c * CHUNK : (c + 1) * CHUNK
-                ]
-
-    def get(ref, index, count):
-        return [ref[(k, *index)] for k in range(count)]
-
-    def put(ref, index, values):
-        for k, value in enumerate(values):
-            ref[(k, *index)] = value
-
-    def own_plane(p, carry):
-        put(prim, (p + 1,), primitive(get(state, (p,), 5)))
-        return carry
-
-    lax.fori_loop(0, planes, own_plane, 0)
-    loads[1].wait()
-
-    def matrices_f(p, carry):
-        jac = half_jacobian(get(prim, (p,), 7))
-        for r in range(5):
-            row = [diag[5 * r + k, p] for k in range(5)]
-            for k, value in enumerate(row_times(row, jac, 1.0)):
-                mats_f[5 * r + k, p] = value
-        return carry
-
-    def matrices_b(p, carry):
-        jac = half_jacobian(get(prim, (p + 2,), 7))
-        for r in range(5):
-            row = [-diag[5 * r + k, p] for k in range(5)]
-            for k, value in enumerate(row_times(row, jac, -1.0)):
-                mats_b[5 * r + k, p] = value
-        return carry
-
-    def multiply(mats, order, out):
-        for n, p in enumerate(order[1:]):
-            final = n == len(order) - 2
-
-            def column(j, carry):
-                if n == 0:
-                    vec = [mats[5 * k + j, order[0]] for k in range(5)]
-                else:
-                    vec = [prod[5 * k + j] for k in range(5)]
-                for r, value in enumerate(mat_vec(lambda e: mats[e, p], vec)):
-                    if final:
-                        pack(out, 5 * r + j, value)
-                    else:
-                        prod[5 * r + j] = value
-                return carry
-
-            lax.fori_loop(0, 5, column, 0)
-
-    lax.fori_loop(1, planes, matrices_f, 0)
+    inner = (me > 0) & (me < last)
+
+    @pl.when(inner)
+    def _():
+        send_some(MAT_F, 1, streams)
+
+    def inner_face(f, carry):
+        put(flux_stream, (f,), roe_twice(get(prim, (f,), 7), get(prim, (f + 1,), 7), 0))
+        return carry
+
+    def span_plane(p, carry):
+        cell = get(prim, (p + 1,), 7)
+        ahead = [pltpu.roll(field, lanes - 1, 1) for field in cell]
+        face = roe_twice(cell, ahead, 2)
+        put(res, (p,), [f - pltpu.roll(f, 1, 1) for f in face])
+        return carry
+
+    lax.fori_loop(0, planes, span_plane, 0)
+    lax.fori_loop(1, planes, inner_face, 0)
     halos[0].wait_recv()
     halos[1].wait_recv()
     below = [jnp.where(me == 0, free_values[k], halo_stream[0, k]) for k in range(5)]
@@ -258,32 +296,10 @@
         jnp.where(me == last, state[k, planes - 1], halo_stream[1, k]) for k in range(5)
     ]
     put(prim, (planes + 1,), primitive(above))
-    matrices_f(0, 0)
-
-    @pl.when((me > 0) & (me < last))
-    def _():
-        multiply(mats_f, list(range(planes)), p_out)
-        send_some(MAT_F, 1, streams)
-        keep_own(MAT_F, 25)
-
-    def inner_face(f, carry):
-        put(flux_stream, (f,), roe_twice(get(prim, (f,), 7), get(prim, (f + 1,), 7), 0))
-        return carry
-
-    lax.fori_loop(0, planes + 1, inner_face, 0)
-
-    def span_plane(p, carry):
-        cell = get(prim, (p + 1,), 7)
-        ahead = [pltpu.roll(field, lanes - 1, 1) for field in cell]
-        face = roe_twice(cell, ahead, 2)
-        put(res, (p,), [f - pltpu.roll(f, 1, 1) for f in face])
-        return carry
-
-    lax.fori_loop(0, planes, span_plane, 0)
+    lax.fori_loop(0, 2, lambda i, c: inner_face(i * planes, c), 0)
     halos[2].wait_recv()
     halos[3].wait_recv()
     loads[2].wait()
-    loads[3].wait()
 
     def ghost(cell, kinds):
         out = []
@@ -296,8 +312,8 @@
 
     row_first = [edge[0, k] for k in range(5)]
     row_last = [edge[1, k] for k in range(5)]
-    ghost_low = ghost(row_first, kinds_low[...])
-    ghost_high = ghost(row_last, kinds_high[...])
+    ghost_low = ghost(row_first, kinds[...] & 3)
+    ghost_high = ghost(row_last, kinds[...] >> 2)
     side_low = [jnp.where(mine == 0, ghost_low[k], halo_cross[0, k]) for k in range(5)]
     side_high = [
         jnp.where(mine == crosses - 1, ghost_high[k], halo_cross[1, k]) for k in range(5)
@@ -326,47 +342,34 @@
         return carry
 
     lax.fori_loop(0, planes, plane_residual, 0)
-    save_res = pltpu.make_async_copy(res, res_hbm, save_sem.at[0])
-    save_res.start()
-
     def plane_drive(p, previous):
-        u, v, s, phi, enth, lam, u1, _, _ = half_jacobian(get(prim, (p,), 7))
-        own = u + lam
-        q = previous[1] - u1 * previous[0]
-        pres = (
-            phi * previous[0]
-            - 0.4 * (u * previous[1] + v * previous[2] + s * previous[3])
-            + 0.2 * previous[4]
-        )
-        term = [
-            0.5 * previous[1] + lam * previous[0],
-            own * previous[1] + u * q + pres,
-            own * previous[2] + v * q,
-            own * previous[3] + s * q,
-            own * previous[4] + u1 * pres + enth * q,
-        ]
+        term = half_apply(half_jacobian(get(prim, (p,), 7)), previous, 1.0)
         out = mat_vec(lambda e: diag[e, p], [term[k] - res[k, p] for k in range(5)])
         put(drive, (p,), out)
         return tuple(out)
 
-    zero = jnp.zeros((rows, lanes), jnp.float32)
-    ahead = lax.fori_loop(0, planes, plane_drive, (zero,) * 5)
+    current = mat_vec(lambda e: diag[e, 0], [-res[k, 0] for k in range(5)])
+    put(drive, (0,), current)
+    current = lax.fori_loop(1, planes, plane_drive, tuple(current))
+    current = half_apply(half_jacobian(get(prim, (planes,), 7)), current, 1.0)
     for k in range(5):
-        pack(a_out, k, ahead[k])
+        pack(a_out, k, current[k])
 
     @pl.when(me < last)
     def _():
         send_some(VEC_F, 1, streams)
-        keep_own(VEC_F, 5)
-
-    lax.fori_loop(0, planes, matrices_b, 0)
+
+    keep_own(MAT_F, 25)
+    keep_own(VEC_F, 5)
+    lax.fori_loop(0, planes - 1, matrices_b, 0)
+    lax.fori_loop(0, 5, product_b, 0)
+    keep_own(MAT_B, 25)
     half = streams // 2
 
-    @pl.when((me > 0) & (me < last))
-    def _():
-        multiply(mats_b, list(reversed(range(planes))), q_out)
+    @pl.when(inner)
+    def _():
+        sent(MAT_F)
         send_some(MAT_B, 1, half)
-        keep_own(MAT_B, 25)
 
     def hand_back(kind, to, values):
         out, into = boxes[kind]
@@ -396,52 +399,45 @@
 
     lax.fori_loop(1, last, scan_f, tuple(current))
 
-    @pl.when((me > 0) & (me < last))
+    @pl.when(inner)
     def _():
         send_some(MAT_B, half, streams)
 
-    def spot(c):
-        return pl.ds(pl.multiple_of(c * CHUNK, CHUNK), CHUNK)
-
-    def gather(kind, c):
-        for i in range(per_chunk):
-            wait_from(kind, c * per_chunk + i)
-
-    def joined(into, c, k):
-        parts = [into[c * per_chunk + i, k] for i in range(per_chunk)]
-        return parts[0] if per_chunk == 1 else jnp.concatenate(parts, axis=0)
-
-    def settle(c, carry):
-        at = spot(c)
-
-        @pl.when(me > 0)
-        def _():
-            gather(BACK_F, c)
-
-        delta = [jnp.where(me == 0, 0.0, joined(s_in, c, k)) for k in range(5)]
-        star = []
-        for p in range(planes):
-            delta = mat_vec(lambda e: mats_f[e, p, :, at], delta)
-            star.append([drive[k, p, :, at] + delta[k] for k in range(5)])
-        current = star[planes - 1]
-        for p in reversed(range(planes)):
-            if p < planes - 1:
-                step = mat_vec(lambda e: mats_b[e, p, :, at], current)
-                current = [star[p][k] + step[k] for k in range(5)]
-            for k in range(5):
-                base[k, p, :, at] = current[k]
-        for i in range(per_chunk):
-            to = c * per_chunk + i
-            for k in range(5):
-                b_out[to, k] = current[k][i * piece : (i + 1) * piece]
-
-            @pl.when((me > 0) & (to != me))
-            def _():
-                outgoing(VEC_B, to).start()
-
-        return carry
-
-    lax.fori_loop(0, chunks, settle, 0)
+    def gather(kind):
+        def one(j, carry):
+            wait_from(kind, j)
+            return carry
+
+        lax.fori_loop(0, streams, one, 0)
+
+    def joined(into, k):
+        wide = []
+        for c in range(chunks):
+            parts = [into[c * per_chunk + i, k] for i in range(per_chunk)]
+            wide.append(parts[0] if per_chunk == 1 else jnp.concatenate(parts, axis=0))
+        return wide[0] if chunks == 1 else jnp.concatenate(wide, axis=1)
+
+    @pl.when(me > 0)
+    def _():
+        gather(BACK_F)
+
+    delta = [jnp.where(me == 0, 0.0, joined(s_in, k)) for k in range(5)]
+    for p in range(planes):
+        delta = mat_vec(lambda e: diag[e, 0] if p == 0 else mats_f[e, p], delta)
+        current = [drive[k, p] + delta[k] for k in range(5)]
+        put(base, (p,), current)
+    for p in reversed(range(planes - 1)):
+        step = mat_vec(lambda e: mats_b[e, p], current)
+        current = [base[k, p] + step[k] for k in range(5)]
+        put(base, (p,), current)
+    current = half_apply(half_jacobian(get(prim, (1,), 7)), current, -1.0)
+    for k in range(5):
+        pack(b_out, k, current[k])
+
+    @pl.when(me > 0)
+    def _():
+        send_some(VEC_B, 1, streams)
+
     keep_own(VEC_B, 5)
 
     wait_from(VEC_B, last)
@@ -459,37 +455,24 @@
 
     lax.fori_loop(1, last, scan_b, tuple(current))
 
-    def finish(c, carry):
-        at = spot(c)
-
-        @pl.when(me < last)
-        def _():
-            gather(BACK_B, c)
-
-        delta = [jnp.where(me == last, 0.0, joined(u_in, c, k)) for k in range(5)]
-        for p in reversed(range(planes)):
-            delta = mat_vec(lambda e: mats_b[e, p, :, at], delta)
-            for k in range(5):
-                upd[k, p, :, at] = base[k, p, :, at] + delta[k]
-        return carry
-
-    lax.fori_loop(0, chunks, finish, 0)
-    save_upd = pltpu.make_async_copy(upd, upd_hbm, save_sem.at[1])
-    save_upd.start()
+    @pl.when(me < last)
+    def _():
+        gather(BACK_B)
+
+    delta = [jnp.where(me == last, 0.0, joined(u_in, k)) for k in range(5)]
+    for p in reversed(range(planes)):
+        if p == planes - 1:
+            delta = [-d for d in mat_vec(lambda e: diag[e, p], delta)]
+        else:
+            delta = mat_vec(lambda e: mats_b[e, p], delta)
+        for k in range(5):
+            upd[k, p] = base[k, p] + delta[k]
 
     for copy in halos:
         copy.wait_send()
 
-    def sent(kind):
-        def one(o, carry):
-            outgoing(kind, lax.rem(me + o, streams)).wait_send()
-            return carry
-
-        lax.fori_loop(1, streams, one, 0)
-
-    @pl.when((me > 0) & (me < last))
-    def _():
-        sent(MAT_F)
+    @pl.when(inner)
+    def _():
         sent(MAT_B)
 
     @pl.when(me < last)
@@ -512,8 +495,6 @@
         return carry
 
     lax.fori_loop(1, streams, sent_back, 0)
-    save_res.wait()
-    save_upd.wait()
 
 
 def local(streams, crosses, state, diag, kinds_low, kinds_high):
@@ -528,12 +509,11 @@
     return pl.pallas_call(
         functools.partial(kernel, streams, crosses),
         out_shape=[jax.ShapeDtypeStruct(state.shape, f32)] * 2,
-        in_specs=[pl.BlockSpec(memory_space=pl.ANY)] * 4,
-        out_specs=[pl.BlockSpec(memory_space=pl.ANY)] * 2,
+        in_specs=[pl.BlockSpec(memory_space=pltpu.HBM)] * 3,
+        out_specs=[pl.BlockSpec(memory_space=pltpu.VMEM)] * 2,
         scratch_shapes=[
             vmem(5, *block),
             vmem(25, *block),
-            pltpu.VMEM((planes, lanes), jnp.int32),
             pltpu.VMEM((planes, lanes), jnp.int32),
             vmem(7, planes + 2, rows, lanes),
             vmem(2, 5, planes, lanes),
@@ -543,28 +523,24 @@
             vmem(5, planes, lanes),
             vmem(5, planes + 1, rows, lanes),
             vmem(5, *block),
-            vmem(5, *block),
             vmem(25, *block),
             vmem(25, *block),
-            vmem(25, rows, lanes),
-            vmem(5, *block),
             vmem(5, *block),
             *[vmem(streams, 25, piece, CHUNK)] * 4,
             *[vmem(streams, 5, piece, CHUNK)] * 8,
-            pltpu.SemaphoreType.DMA((4,)),
-            pltpu.SemaphoreType.DMA((2,)),
+            pltpu.SemaphoreType.DMA((3,)),
             pltpu.SemaphoreType.DMA((4,)),
             pltpu.SemaphoreType.DMA((4,)),
             pltpu.SemaphoreType.DMA((6, streams)),
             pltpu.SemaphoreType.DMA((6, streams)),
         ],
         compiler_params=pltpu.CompilerParams(
-            collective_id=0, has_side_effects=True, vmem_limit_bytes=60 * 2**20
+            collective_id=0, has_side_effects=True, vmem_limit_bytes=54400 * 1024
         ),
         cost_estimate=pl.CostEstimate(
             flops=16000000, bytes_accessed=2700000, transcendentals=100000
         ),
-    )(state, diag, kinds_low, kinds_high)
+    )(state, diag, kinds_low + 4 * kinds_high)
 
 
 def solution(mesh):

time: 56.9 us -> 52.1 us (0.916); the launches traced: 55.8 us -> 51.9 us
  Pallas kernels: 51.7 us -> 49.1 us
  local copies, waits for them, and re-layouts: 3.45 us -> 1.45 us
  other arithmetic: 0 us -> 0.72 us
    pallas_call x1, Pallas kernels: 51.7 us -> 49.1 us  [local(): pl.pallas_call(functools.partial(kernel, streams, crosses), out_shape=[ja...]
    unnamed x2, local copies, waits for them, and re-layouts: 3.45 us -> 1.45 us
    add x0 -> x1, other arithmetic: none -> 0.72 us  [local(): kinds_low + 4 * kinds_high]
where the time goes in v2:
time: 52.1 us; the launch traced here: 51.9 us
  Pallas kernels  49.1 us (94%)
  local copies, waits for them, and re-layouts  1.45 us (3%)
  other arithmetic  0.72 us (1%)
  between operations  0.64 us (1%)
    pallas_call x1, Pallas kernels, local(): pl.pallas_call(functools.partial(kernel, streams, crosses), out_shape=[ja...  49.1 us
    unnamed x2, local copies, waits for them, and re-layouts  1.45 us

profile of v2, /device:TPU:56, one launch (start us, length us, event | category | flops | bytes accessed | tf_op | source)
XLA Modules:
  0.0 51.9 jit_solution(17663415090323402191)
XLA Ops:
  0.6 0.7 %multiply_add_fusion.kinds_hbm = s32[4,512]{1,0:T(4,128)S(1)} fusion(s32[4,512]{1,0:T(4,128)} %param.6, s32[4,512]{1,0:T(4,128)} %param.7), kind=kLoop, calls=%fused_computation | loop fusion | flops 4096 | bytes 24576 | tf_op jit(solution)/shard_map/add | solution.py:543
  1.4 49.1 %shard_map.59 = (f32[5,4,8,512]{3,2,1,0:T(8,128)S(1)}, f32[5,4,8,512]{3,2,1,0:T(8,128)S(1)}) custom-call(f32[5,4,8,512]{3,2,1,0:T(8,128)} %state_hbm.1, f32[25,4,8,512]{3,2,1,0:T(8,128)} %diag_hbm.1, s32[4,512]{1,0:T(4,128)S(1)} %multiply_add_fusion.kinds_hbm), custom_call_target="tpu_custom_call" | custom-call | flops 16000000 | bytes 2700000 | tf_op jit(solution)/shard_map/pallas_call | solution.py:509
  50.4 0.7 %copy.8 = f32[5,4,8,512]{3,2,1,0:T(8,128)} copy(f32[5,4,8,512]{3,2,1,0:T(8,128)S(1)} %get-tuple-element.4) | data formatting | bytes 655360
  51.2 0.7 %copy.9 = f32[5,4,8,512]{3,2,1,0:T(8,128)} copy(f32[5,4,8,512]{3,2,1,0:T(8,128)S(1)} %get-tuple-element.5) | data formatting | bytes 655360

commit v3 on v2

--- a/solution.py
+++ b/solution.py
@@ -260,14 +260,29 @@
 
         lax.fori_loop(1, streams, one, 0)
 
-    def keep_own(kind, count):
+    def keep_own(kind):
         out, into = boxes[kind]
-
-        def one(e, carry):
-            into[me, e] = out[me, e]
+        into[me] = out[me]
+
+    def gather(kind, first, end):
+        def one(j, carry):
+            wait_from(kind, j)
             return carry
 
-        lax.fori_loop(0, count, one, 0)
+        lax.fori_loop(first, end, one, 0)
+
+    def hand_back(kind, skip):
+        def one(o, carry):
+            to = lax.rem(me + o, streams)
+
+            @pl.when(to != skip)
+            def _():
+                outgoing(kind, to).start()
+
+            return carry
+
+        lax.fori_loop(1, streams, one, 0)
+        keep_own(kind)
 
     inner = (me > 0) & (me < last)
 
@@ -359,11 +374,11 @@
     def _():
         send_some(VEC_F, 1, streams)
 
-    keep_own(MAT_F, 25)
-    keep_own(VEC_F, 5)
+    keep_own(MAT_F)
+    keep_own(VEC_F)
     lax.fori_loop(0, planes - 1, matrices_b, 0)
     lax.fori_loop(0, 5, product_b, 0)
-    keep_own(MAT_B, 25)
+    keep_own(MAT_B)
     half = streams // 2
 
     @pl.when(inner)
@@ -371,44 +386,20 @@
         sent(MAT_F)
         send_some(MAT_B, 1, half)
 
-    def hand_back(kind, to, values):
-        out, into = boxes[kind]
+    gather(MAT_F, 1, last)
+    gather(VEC_F, 0, last)
+    current = [a_in[0, k] for k in range(5)]
+    for j in range(1, streams):
         for k in range(5):
-            out[to, k] = values[k]
-
-        @pl.when(to != me)
-        def _():
-            outgoing(kind, to).start()
-
-        @pl.when(to == me)
-        def _():
-            for k in range(5):
-                into[me, k] = values[k]
-
-    wait_from(VEC_F, 0)
-    current = [a_in[0, k] for k in range(5)]
-    hand_back(BACK_F, 1, current)
-
-    def scan_f(j, vec):
-        wait_from(MAT_F, j)
-        wait_from(VEC_F, j)
-        step = mat_vec(lambda e: p_in[j, e], vec)
-        out = [a_in[j, k] + step[k] for k in range(5)]
-        hand_back(BACK_F, j + 1, out)
-        return tuple(out)
-
-    lax.fori_loop(1, last, scan_f, tuple(current))
+            s_out[j, k] = current[k]
+        if j < last:
+            step = mat_vec(lambda e: p_in[j, e], current)
+            current = [a_in[j, k] + step[k] for k in range(5)]
+    hand_back(BACK_F, 0)
 
     @pl.when(inner)
     def _():
         send_some(MAT_B, half, streams)
-
-    def gather(kind):
-        def one(j, carry):
-            wait_from(kind, j)
-            return carry
-
-        lax.fori_loop(0, streams, one, 0)
 
     def joined(into, k):
         wide = []
@@ -419,7 +410,7 @@
 
     @pl.when(me > 0)
     def _():
-        gather(BACK_F)
+        gather(BACK_F, 0, streams)
 
     delta = [jnp.where(me == 0, 0.0, joined(s_in, k)) for k in range(5)]
     for p in range(planes):
@@ -438,26 +429,22 @@
     def _():
         send_some(VEC_B, 1, streams)
 
-    keep_own(VEC_B, 5)
-
-    wait_from(VEC_B, last)
+    keep_own(VEC_B)
+
+    gather(MAT_B, 1, last)
+    gather(VEC_B, 1, streams)
     current = [b_in[last, k] for k in range(5)]
-    hand_back(BACK_B, last - 1, current)
-
-    def scan_b(n, vec):
-        j = last - n
-        wait_from(MAT_B, j)
-        wait_from(VEC_B, j)
-        step = mat_vec(lambda e: q_in[j, e], vec)
-        out = [b_in[j, k] + step[k] for k in range(5)]
-        hand_back(BACK_B, j - 1, out)
-        return tuple(out)
-
-    lax.fori_loop(1, last, scan_b, tuple(current))
+    for j in reversed(range(last)):
+        for k in range(5):
+            u_out[j, k] = current[k]
+        if j > 0:
+            step = mat_vec(lambda e: q_in[j, e], current)
+            current = [b_in[j, k] + step[k] for k in range(5)]
+    hand_back(BACK_B, last)
 
     @pl.when(me < last)
     def _():
-        gather(BACK_B)
+        gather(BACK_B, 0, streams)
 
     delta = [jnp.where(me == last, 0.0, joined(u_in, k)) for k in range(5)]
     for p in reversed(range(planes)):

time: 52.1 us -> 53.9 us (1.035)
  Pallas kernels: 49.1 us -> 50.9 us
    pallas_call x1, Pallas kernels: 49.1 us -> 50.9 us  [local(): pl.pallas_call(functools.partial(kernel, streams, crosses), out_shape=[ja...]
where the time goes in v3:
time: 53.9 us; the launch traced here: 53.7 us
  Pallas kernels  50.9 us (94%)
  local copies, waits for them, and re-layouts  1.45 us (3%)
  other arithmetic  0.72 us (1%)
  between operations  0.64 us (1%)
    pallas_call x1, Pallas kernels, local(): pl.pallas_call(functools.partial(kernel, streams, crosses), out_shape=[ja...  50.9 us
    unnamed x2, local copies, waits for them, and re-layouts  1.45 us

profile of v3, /device:TPU:56, one launch (start us, length us, event | category | flops | bytes accessed | tf_op | source)
XLA Modules:
  0.0 53.7 jit_solution(11494419681544120632)
XLA Ops:
  0.6 0.7 %multiply_add_fusion.kinds_hbm = s32[4,512]{1,0:T(4,128)S(1)} fusion(s32[4,512]{1,0:T(4,128)} %param.6, s32[4,512]{1,0:T(4,128)} %param.7), kind=kLoop, calls=%fused_computation | loop fusion | flops 4096 | bytes 24576 | tf_op jit(solution)/shard_map/add | solution.py:530
  1.4 50.9 %shard_map.59 = (f32[5,4,8,512]{3,2,1,0:T(8,128)S(1)}, f32[5,4,8,512]{3,2,1,0:T(8,128)S(1)}) custom-call(f32[5,4,8,512]{3,2,1,0:T(8,128)} %state_hbm.1, f32[25,4,8,512]{3,2,1,0:T(8,128)} %diag_hbm.1, s32[4,512]{1,0:T(4,128)S(1)} %multiply_add_fusion.kinds_hbm), custom_call_target="tpu_custom_call" | custom-call | flops 16000000 | bytes 2700000 | tf_op jit(solution)/shard_map/pallas_call | solution.py:496
  52.3 0.7 %copy.8 = f32[5,4,8,512]{3,2,1,0:T(8,128)} copy(f32[5,4,8,512]{3,2,1,0:T(8,128)S(1)} %get-tuple-element.4) | data formatting | bytes 655360
  53.0 0.7 %copy.9 = f32[5,4,8,512]{3,2,1,0:T(8,128)} copy(f32[5,4,8,512]{3,2,1,0:T(8,128)S(1)} %get-tuple-element.5) | data formatting | bytes 655360

commit v4 on v2

--- a/solution.py
+++ b/solution.py
@@ -113,7 +113,7 @@
     state, diag, kinds, prim, edge, halo_cross, halo_stream, low_prim, top_flux,
     flux_stream, drive, mats_f, mats_b, base,
     p_out, p_in, q_out, q_in, a_out, a_in, s_out, s_in, b_out, b_in, u_out, u_in,
-    load_sem, halo_send, halo_recv, sends, recvs,
+    passed, load_sem, halo_send, halo_recv, sends, recvs, first_recv, second_send,
 ):
     me = lax.axis_index("stream")
     mine = lax.axis_index("cross")
@@ -260,20 +260,71 @@
 
         lax.fori_loop(1, streams, one, 0)
 
-    def keep_own(kind, count):
+    def keep_own(kind):
         out, into = boxes[kind]
-
-        def one(e, carry):
-            into[me, e] = out[me, e]
+        into[me] = out[me]
+
+    inner = (me > 0) & (me < last)
+
+    ring = streams // 2
+    corner = ring // 4
+
+    def around(by):
+        return (me // ring) * ring + lax.rem(lax.rem(me, ring) + by, ring)
+
+    def first_leg(kind, way):
+        to = lax.rem(me + (ring // 2, streams - ring // 2)[way], streams)
+        middle = around((corner, ring - corner)[way])
+        slot = (kind // 3) * 2 + way
+        return remote(
+            boxes[kind][0].at[to], passed.at[slot], sends.at[kind, to], first_recv.at[slot],
+            {"stream": middle},
+        )
+
+    def second_leg(kind, way):
+        origin = around((ring - corner, corner)[way])
+        to = lax.rem(origin + (ring // 2, streams - ring // 2)[way], streams)
+        slot = (kind // 3) * 2 + way
+        return origin, remote(
+            passed.at[slot], boxes[kind][1].at[origin], second_send.at[slot],
+            recvs.at[kind, origin], {"stream": to},
+        )
+
+    def start_first(kind):
+        for way in range(2):
+            first_leg(kind, way).start()
+
+    def pass_on(kind):
+        for way in range(2):
+            origin, copy = second_leg(kind, way)
+
+            @pl.when((origin > 0) & (origin < last))
+            def _():
+                first_leg(kind, way).wait_recv()
+                copy.start()
+
+    def passed_on(kind):
+        for way in range(2):
+            origin, copy = second_leg(kind, way)
+
+            @pl.when((origin > 0) & (origin < last))
+            def _():
+                copy.wait_send()
+
+    def send_matrices(kind, first, end):
+        def one(o, carry):
+            @pl.when(lax.rem(o, ring) != ring // 2)
+            def _():
+                outgoing(kind, lax.rem(me + o, streams)).start()
+
             return carry
 
-        lax.fori_loop(0, count, one, 0)
-
-    inner = (me > 0) & (me < last)
+        lax.fori_loop(first, end, one, 0)
 
     @pl.when(inner)
     def _():
-        send_some(MAT_F, 1, streams)
+        start_first(MAT_F)
+        send_matrices(MAT_F, 1, streams)
 
     def inner_face(f, carry):
         put(flux_stream, (f,), roe_twice(get(prim, (f,), 7), get(prim, (f + 1,), 7), 0))
@@ -297,6 +348,7 @@
     ]
     put(prim, (planes + 1,), primitive(above))
     lax.fori_loop(0, 2, lambda i, c: inner_face(i * planes, c), 0)
+    pass_on(MAT_F)
     halos[2].wait_recv()
     halos[3].wait_recv()
     loads[2].wait()
@@ -359,17 +411,18 @@
     def _():
         send_some(VEC_F, 1, streams)
 
-    keep_own(MAT_F, 25)
-    keep_own(VEC_F, 5)
+    keep_own(MAT_F)
+    keep_own(VEC_F)
     lax.fori_loop(0, planes - 1, matrices_b, 0)
     lax.fori_loop(0, 5, product_b, 0)
-    keep_own(MAT_B, 25)
+    keep_own(MAT_B)
     half = streams // 2
 
     @pl.when(inner)
     def _():
         sent(MAT_F)
-        send_some(MAT_B, 1, half)
+        start_first(MAT_B)
+        send_matrices(MAT_B, 1, half - 1)
 
     def hand_back(kind, to, values):
         out, into = boxes[kind]
@@ -399,9 +452,11 @@
 
     lax.fori_loop(1, last, scan_f, tuple(current))
 
+    pass_on(MAT_B)
+
     @pl.when(inner)
     def _():
-        send_some(MAT_B, half, streams)
+        send_matrices(MAT_B, half - 1, streams)
 
     def gather(kind):
         def one(j, carry):
@@ -438,7 +493,7 @@
     def _():
         send_some(VEC_B, 1, streams)
 
-    keep_own(VEC_B, 5)
+    keep_own(VEC_B)
 
     wait_from(VEC_B, last)
     current = [b_in[last, k] for k in range(5)]
@@ -474,6 +529,9 @@
     @pl.when(inner)
     def _():
         sent(MAT_B)
+
+    passed_on(MAT_F)
+    passed_on(MAT_B)
 
     @pl.when(me < last)
     def _():
@@ -528,11 +586,14 @@
             vmem(5, *block),
             *[vmem(streams, 25, piece, CHUNK)] * 4,
             *[vmem(streams, 5, piece, CHUNK)] * 8,
+            vmem(4, 25, piece, CHUNK),
             pltpu.SemaphoreType.DMA((3,)),
             pltpu.SemaphoreType.DMA((4,)),
             pltpu.SemaphoreType.DMA((4,)),
             pltpu.SemaphoreType.DMA((6, streams)),
             pltpu.SemaphoreType.DMA((6, streams)),
+            pltpu.SemaphoreType.DMA((4,)),
+            pltpu.SemaphoreType.DMA((4,)),
         ],
         compiler_params=pltpu.CompilerParams(
             collective_id=0, has_side_effects=True, vmem_limit_bytes=54400 * 1024

time: 52.1 us -> 52 us (level)
  no operation moved by 1% of the time
where the time goes in v4:
time: 52 us; the launch traced here: 51.4 us
  Pallas kernels  48.6 us (93%)
  local copies, waits for them, and re-layouts  1.45 us (3%)
  other arithmetic  0.72 us (1%)
  between operations  0.64 us (1%)
    pallas_call x1, Pallas kernels, local(): pl.pallas_call(functools.partial(kernel, streams, crosses), out_shape=[ja...  48.6 us
    unnamed x2, local copies, waits for them, and re-layouts  1.45 us

profile of v4, /device:TPU:56, one launch (start us, length us, event | category | flops | bytes accessed | tf_op | source)
XLA Modules:
  0.0 51.4 jit_solution(10452528248467910952)
XLA Ops:
  0.6 0.7 %multiply_add_fusion.kinds_hbm = s32[4,512]{1,0:T(4,128)S(1)} fusion(s32[4,512]{1,0:T(4,128)} %param.6, s32[4,512]{1,0:T(4,128)} %param.7), kind=kLoop, calls=%fused_computation | loop fusion | flops 4096 | bytes 24576 | tf_op jit(solution)/shard_map/add | solution.py:604
  1.4 48.6 %shard_map.59 = (f32[5,4,8,512]{3,2,1,0:T(8,128)S(1)}, f32[5,4,8,512]{3,2,1,0:T(8,128)S(1)}) custom-call(f32[5,4,8,512]{3,2,1,0:T(8,128)} %state_hbm.1, f32[25,4,8,512]{3,2,1,0:T(8,128)} %diag_hbm.1, s32[4,512]{1,0:T(4,128)S(1)} %multiply_add_fusion.kinds_hbm), custom_call_target="tpu_custom_call" | custom-call | flops 16000000 | bytes 2700000 | tf_op jit(solution)/shard_map/pallas_call | solution.py:567
  50.0 0.7 %copy.8 = f32[5,4,8,512]{3,2,1,0:T(8,128)} copy(f32[5,4,8,512]{3,2,1,0:T(8,128)S(1)} %get-tuple-element.4) | data formatting | bytes 655360
  50.7 0.7 %copy.9 = f32[5,4,8,512]{3,2,1,0:T(8,128)} copy(f32[5,4,8,512]{3,2,1,0:T(8,128)S(1)} %get-tuple-element.5) | data formatting | bytes 655360

commit v5 on v2

--- a/solution.py
+++ b/solution.py
@@ -111,7 +111,7 @@
     streams, crosses,
     state_hbm, diag_hbm, kinds_hbm, res, upd,
     state, diag, kinds, prim, edge, halo_cross, halo_stream, low_prim, top_flux,
-    flux_stream, drive, mats_f, mats_b, base,
+    flux_stream, drive, mats_f, mats_b, base, back,
     p_out, p_in, q_out, q_in, a_out, a_in, s_out, s_in, b_out, b_in, u_out, u_in,
     load_sem, halo_send, halo_recv, sends, recvs,
 ):
@@ -246,12 +246,12 @@
                 recvs.at[kind, source], {"stream": source},
             ).wait_recv()
 
+    ring = streams // 2
+    offsets = sorted(range(1, streams), key=lambda o: -min(o % ring, ring - o % ring))
+
     def send_some(kind, first, end):
-        def one(o, carry):
+        for o in offsets[first:end]:
             outgoing(kind, lax.rem(me + o, streams)).start()
-            return carry
-
-        lax.fori_loop(first, end, one, 0)
 
     def sent(kind):
         def one(o, carry):
@@ -260,20 +260,15 @@
 
         lax.fori_loop(1, streams, one, 0)
 
-    def keep_own(kind, count):
+    def keep_own(kind):
         out, into = boxes[kind]
-
-        def one(e, carry):
-            into[me, e] = out[me, e]
-            return carry
-
-        lax.fori_loop(0, count, one, 0)
+        into[me] = out[me]
 
     inner = (me > 0) & (me < last)
 
     @pl.when(inner)
     def _():
-        send_some(MAT_F, 1, streams)
+        send_some(MAT_F, 0, last)
 
     def inner_face(f, carry):
         put(flux_stream, (f,), roe_twice(get(prim, (f,), 7), get(prim, (f + 1,), 7), 0))
@@ -357,19 +352,42 @@
 
     @pl.when(me < last)
     def _():
-        send_some(VEC_F, 1, streams)
-
-    keep_own(MAT_F, 25)
-    keep_own(VEC_F, 5)
+        send_some(VEC_F, 0, last)
+
+    keep_own(MAT_F)
+    keep_own(VEC_F)
     lax.fori_loop(0, planes - 1, matrices_b, 0)
     lax.fori_loop(0, 5, product_b, 0)
-    keep_own(MAT_B, 25)
+
+    def back_down(column, current):
+        for p in reversed(range(planes - 1)):
+            step = mat_vec(lambda e: mats_b[e, p], current)
+            current = [column(k, p) + step[k] for k in range(5)]
+        return half_apply(half_jacobian(get(prim, (1,), 7)), current, -1.0)
+
+    for k, value in enumerate(
+        back_down(lambda k, p: drive[k, p], get(drive, (planes - 1,), 5))
+    ):
+        back[25 + k] = value
+
+    def back_column(j, carry):
+        delta = [diag[5 * k + j, 0] for k in range(5)]
+        put(base, (0,), delta)
+        for p in range(1, planes):
+            delta = mat_vec(lambda e: mats_f[e, p], delta)
+            put(base, (p,), delta)
+        for r, value in enumerate(back_down(lambda k, p: base[k, p], delta)):
+            back[5 * r + j] = value
+        return carry
+
+    lax.fori_loop(0, 5, back_column, 0)
+    keep_own(MAT_B)
     half = streams // 2
 
     @pl.when(inner)
     def _():
         sent(MAT_F)
-        send_some(MAT_B, 1, half)
+        send_some(MAT_B, 0, half - 1)
 
     def hand_back(kind, to, values):
         out, into = boxes[kind]
@@ -401,7 +419,7 @@
 
     @pl.when(inner)
     def _():
-        send_some(MAT_B, half, streams)
+        send_some(MAT_B, half - 1, last)
 
     def gather(kind):
         def one(j, carry):
@@ -421,7 +439,17 @@
     def _():
         gather(BACK_F)
 
-    delta = [jnp.where(me == 0, 0.0, joined(s_in, k)) for k in range(5)]
+    incoming = [jnp.where(me == 0, 0.0, joined(s_in, k)) for k in range(5)]
+    step = mat_vec(lambda e: back[e], incoming)
+    for k in range(5):
+        pack(b_out, k, back[25 + k] + step[k])
+
+    @pl.when(me > 0)
+    def _():
+        send_some(VEC_B, 0, last)
+
+    keep_own(VEC_B)
+    delta = incoming
     for p in range(planes):
         delta = mat_vec(lambda e: diag[e, 0] if p == 0 else mats_f[e, p], delta)
         current = [drive[k, p] + delta[k] for k in range(5)]
@@ -430,15 +458,6 @@
         step = mat_vec(lambda e: mats_b[e, p], current)
         current = [base[k, p] + step[k] for k in range(5)]
         put(base, (p,), current)
-    current = half_apply(half_jacobian(get(prim, (1,), 7)), current, -1.0)
-    for k in range(5):
-        pack(b_out, k, current[k])
-
-    @pl.when(me > 0)
-    def _():
-        send_some(VEC_B, 1, streams)
-
-    keep_own(VEC_B, 5)
 
     wait_from(VEC_B, last)
     current = [b_in[last, k] for k in range(5)]
@@ -497,6 +516,17 @@
     lax.fori_loop(1, streams, sent_back, 0)
 
 
+def store(res, upd, res_out, upd_out, sem):
+    copies = [
+        pltpu.make_async_copy(src, dst, sem.at[i])
+        for i, (src, dst) in enumerate([(res, res_out), (upd, upd_out)])
+    ]
+    for copy in copies:
+        copy.start()
+    for copy in copies:
+        copy.wait()
+
+
 def local(streams, crosses, state, diag, kinds_low, kinds_high):
     _, planes, rows, lanes = state.shape
     piece = rows * (lanes // CHUNK) // streams
@@ -506,7 +536,7 @@
     def vmem(*shape):
         return pltpu.VMEM(shape, f32)
 
-    return pl.pallas_call(
+    residual, update = pl.pallas_call(
         functools.partial(kernel, streams, crosses),
         out_shape=[jax.ShapeDtypeStruct(state.shape, f32)] * 2,
         in_specs=[pl.BlockSpec(memory_space=pltpu.HBM)] * 3,
@@ -526,6 +556,7 @@
             vmem(25, *block),
             vmem(25, *block),
             vmem(5, *block),
+            vmem(30, rows, lanes),
             *[vmem(streams, 25, piece, CHUNK)] * 4,
             *[vmem(streams, 5, piece, CHUNK)] * 8,
             pltpu.SemaphoreType.DMA((3,)),
@@ -541,6 +572,14 @@
             flops=16000000, bytes_accessed=2700000, transcendentals=100000
         ),
     )(state, diag, kinds_low + 4 * kinds_high)
+    return pl.pallas_call(
+        store,
+        out_shape=[jax.ShapeDtypeStruct(state.shape, f32)] * 2,
+        in_specs=[pl.BlockSpec(memory_space=pl.ANY)] * 2,
+        out_specs=[pl.BlockSpec(memory_space=pl.ANY)] * 2,
+        scratch_shapes=[pltpu.SemaphoreType.DMA((2,))],
+        cost_estimate=pl.CostEstimate(flops=0, bytes_accessed=1310720, transcendentals=0),
+    )(residual, update)
 
 
 def solution(mesh):

time: 52.1 us -> 73.2 us (1.40)
  Pallas kernels: 49.1 us -> 70 us
    pallas_call x0 -> x1, Pallas kernels: none -> 21 us  [local(): pl.pallas_call(store, out_shape=[jax.ShapeDtypeStruct(state.shape, f32)]...]
where the time goes in v5:
time: 73.2 us; the launch traced here: 72.8 us
  Pallas kernels  70 us (96%)
  local copies, waits for them, and re-layouts  1.43 us (2%)
    pallas_call x1, Pallas kernels, local(): pl.pallas_call(functools.partial(kernel, streams, crosses), out_shape=[ja...  49.1 us
    pallas_call x1, Pallas kernels, local(): pl.pallas_call(store, out_shape=[jax.ShapeDtypeStruct(state.shape, f32)]...  21 us

profile of v5, /device:TPU:56, one launch (start us, length us, event | category | flops | bytes accessed | tf_op | source)
XLA Modules:
  0.0 72.8 jit_solution(5233713464325144927)
XLA Ops:
  0.6 0.7 multiply_add_fusion.kinds_hbm
  1.4 49.1 %shard_map.59 = (f32[5,4,8,512]{3,2,1,0:T(8,128)S(1)}, f32[5,4,8,512]{3,2,1,0:T(8,128)S(1)}) custom-call(f32[5,4,8,512]{3,2,1,0:T(8,128)} %state_hbm.1, f32[25,4,8,512]{3,2,1,0:T(8,128)} %diag_hbm.1, s32[4,512]{1,0:T(4,128)S(1)} %multiply_add_fusion.kinds_hbm), custom_call_target="tpu_custom_call" | custom-call | flops 16000000 | bytes 2700000 | tf_op jit(solution)/shard_map/pallas_call | solution.py:539
  50.4 0.0 copy-start
  50.4 0.7 copy-done
  51.1 0.0 copy-start.1
  51.1 0.7 copy-done.1
  51.9 21.0 %shard_map.60 = (f32[5,4,8,512]{3,2,1,0:T(8,128)}, f32[5,4,8,512]{3,2,1,0:T(8,128)}) custom-call(f32[5,4,8,512]{3,2,1,0:T(8,128)} %copy-done, f32[5,4,8,512]{3,2,1,0:T(8,128)} %copy-done.1), custom_call_target="tpu_custom_call" | custom-call | bytes 1310720 | tf_op jit(solution)/shard_map/pallas_call | solution.py:575
Async XLA Ops:
  50.4 0.7 copy-start
  51.1 0.7 copy-start.1

commit v6 on v2

--- a/solution.py
+++ b/solution.py
@@ -364,12 +364,11 @@
     lax.fori_loop(0, planes - 1, matrices_b, 0)
     lax.fori_loop(0, 5, product_b, 0)
     keep_own(MAT_B, 25)
-    half = streams // 2
 
     @pl.when(inner)
     def _():
         sent(MAT_F)
-        send_some(MAT_B, 1, half)
+        send_some(MAT_B, 1, streams)
 
     def hand_back(kind, to, values):
         out, into = boxes[kind]
@@ -398,10 +397,6 @@
         return tuple(out)
 
     lax.fori_loop(1, last, scan_f, tuple(current))
-
-    @pl.when(inner)
-    def _():
-        send_some(MAT_B, half, streams)
 
     def gather(kind):
         def one(j, carry):

time: 52.1 us -> 53.7 us (1.031)
  Pallas kernels: 49.1 us -> 50.6 us
    pallas_call x1, Pallas kernels: 49.1 us -> 50.6 us  [local(): pl.pallas_call(functools.partial(kernel, streams, crosses), out_shape=[ja...]
where the time goes in v6:
time: 53.7 us; the launch traced here: 53.5 us
  Pallas kernels  50.6 us (94%)
  local copies, waits for them, and re-layouts  1.45 us (3%)
  other arithmetic  0.72 us (1%)
  between operations  0.64 us (1%)
    pallas_call x1, Pallas kernels, local(): pl.pallas_call(functools.partial(kernel, streams, crosses), out_shape=[ja...  50.6 us
    unnamed x2, local copies, waits for them, and re-layouts  1.45 us

profile of v6, /device:TPU:56, one launch (start us, length us, event | category | flops | bytes accessed | tf_op | source)
XLA Modules:
  0.0 53.5 jit_solution(449468666728518789)
XLA Ops:
  0.6 0.7 %multiply_add_fusion.kinds_hbm = s32[4,512]{1,0:T(4,128)S(1)} fusion(s32[4,512]{1,0:T(4,128)} %param.6, s32[4,512]{1,0:T(4,128)} %param.7), kind=kLoop, calls=%fused_computation | loop fusion | flops 4096 | bytes 24576 | tf_op jit(solution)/shard_map/add | solution.py:538
  1.4 50.6 %shard_map.59 = (f32[5,4,8,512]{3,2,1,0:T(8,128)S(1)}, f32[5,4,8,512]{3,2,1,0:T(8,128)S(1)}) custom-call(f32[5,4,8,512]{3,2,1,0:T(8,128)} %state_hbm.1, f32[25,4,8,512]{3,2,1,0:T(8,128)} %diag_hbm.1, s32[4,512]{1,0:T(4,128)S(1)} %multiply_add_fusion.kinds_hbm), custom_call_target="tpu_custom_call" | custom-call | flops 16000000 | bytes 2700000 | tf_op jit(solution)/shard_map/pallas_call | solution.py:504
  52.0 0.7 %copy.8 = f32[5,4,8,512]{3,2,1,0:T(8,128)} copy(f32[5,4,8,512]{3,2,1,0:T(8,128)S(1)} %get-tuple-element.4) | data formatting | bytes 655360
  52.7 0.7 %copy.9 = f32[5,4,8,512]{3,2,1,0:T(8,128)} copy(f32[5,4,8,512]{3,2,1,0:T(8,128)S(1)} %get-tuple-element.5) | data formatting | bytes 655360
